TPU v7x, 256 devices: a whole 4x4x8 slice. The times are simulated.
256 devices in a mesh: expert: 16 (over x, z_lo, core), fsdp: 4 (over y), dp: 4 (over z_hi).
Axes of the slice: x: 4, y: 4, z: 8 (z_hi: 4, z_lo: 2; z = z_hi * 2 + z_lo), core: 2. Of those that a mesh axis runs over, the one named last changes fastest.
Arguments:
- inputs: bfloat16 [24576, 2048], P(('expert', 'fsdp', 'dp')), may hold values from -6 to 6
- upstream: bfloat16 [24576, 2048], P(('expert', 'fsdp', 'dp')), may hold values from -6 to 6
- gates: float32 [24576, 2], P(('expert', 'fsdp', 'dp')), may hold values from 0.2 to 1
- routes: int32 [24576, 2], P(('expert', 'fsdp', 'dp')), may hold values from 0 to 15, all different within a row; in each aligned block of 96 rows (0 to 95, 96 to 191, ...) at most 36 rows name the same one
- w_gate: bfloat16 [16, 768, 2048], P('expert', 'fsdp'), may hold values from -0.125 to 0.125
- w_up: bfloat16 [16, 768, 2048], P('expert', 'fsdp'), may hold values from -0.125 to 0.125
- w_down: bfloat16 [16, 768, 2048], P('expert', 'fsdp'), may hold values from -0.21875 to 0.21875
Outputs:
- grad_inputs: bfloat16 [24576, 2048], P(('expert', 'fsdp', 'dp'))
- grad_gate: bfloat16 [16, 768, 2048], P('expert', 'fsdp')
- grad_up: bfloat16 [16, 768, 2048], P('expert', 'fsdp')
- grad_down: bfloat16 [16, 768, 2048], P('expert', 'fsdp')
Inputs may be any that keep to these rules, and one draw needn't show every extreme that they name: `routes`: each row names 2 different experts. Among the 96 rows of one device no expert is named more than 36 times, and on some device some expert is named exactly 36 times.
All inputs are finite; a program needn't handle non-finite values.
Results may differ from a plain program's by a relative error of at most 0.018.
Values may be sent and summed in bfloat16 or wider, within the bound.
A program may use at most 128 MiB of HBM per device.

v0:
```python
import jax
import jax.numpy as jnp
from jax import lax
from jax.sharding import PartitionSpec as P


def route_table(routes, experts, capacity):
    route_list = routes.reshape(-1)
    member = (route_list[:, None] == jnp.arange(experts, dtype=jnp.int32)[None, :]).astype(
        jnp.int32
    )
    earlier = jnp.cumsum(member, axis=0) - member
    position = jnp.sum(earlier * member, axis=1)
    target = route_list * capacity + position
    hits = jnp.arange(experts * capacity, dtype=jnp.int32)[:, None] == target[None, :]
    return hits.reshape(experts * capacity, routes.shape[0], routes.shape[1])


def dispatch(inputs, upstream, gates, routes, experts, capacity):
    hits = route_table(routes, experts, capacity)
    token_table = jnp.sum(hits.astype(jnp.int32), axis=2).astype(jnp.bfloat16)
    gate_table = jnp.sum(
        jnp.where(hits, gates[None, :, :], jnp.zeros_like(gates)[None, :, :]), axis=2
    )
    sent_inputs = jnp.dot(token_table, inputs, preferred_element_type=jnp.float32).astype(
        jnp.bfloat16
    )
    sent_scaled = jnp.dot(
        gate_table, upstream.astype(jnp.float32), precision=lax.Precision.HIGHEST
    ).astype(jnp.bfloat16)
    return (sent_inputs, sent_scaled, token_table)


def block_backward(rows_in, rows_scaled, gate_block, up_block, down_block):
    contract_last = (((1,), (1,)), ((), ()))
    contract_first = (((0,), (0,)), ((), ()))
    gate = lax.dot_general(rows_in, gate_block, contract_last, preferred_element_type=jnp.float32)
    upward = lax.dot_general(rows_in, up_block, contract_last, preferred_element_type=jnp.float32)
    logistic = jax.nn.sigmoid(gate)
    active = gate * logistic
    slope = logistic * (1.0 + gate * (1.0 - logistic))
    hidden = (active * upward).astype(jnp.bfloat16)
    d_hidden = lax.dot_general(
        rows_scaled, down_block, contract_last, preferred_element_type=jnp.float32
    )
    d_up = (d_hidden * active).astype(jnp.bfloat16)
    d_gate = (d_hidden * upward * slope).astype(jnp.bfloat16)
    grad_down = lax.dot_general(
        hidden, rows_scaled, contract_first, preferred_element_type=jnp.float32
    )
    grad_up = lax.dot_general(d_up, rows_in, contract_first, preferred_element_type=jnp.float32)
    grad_gate = lax.dot_general(d_gate, rows_in, contract_first, preferred_element_type=jnp.float32)
    term = jnp.dot(d_gate, gate_block, preferred_element_type=jnp.float32) + jnp.dot(
        d_up, up_block, preferred_element_type=jnp.float32
    )
    return (term, grad_gate, grad_up, grad_down)


def rounded(value):
    return lax.optimization_barrier(value.astype(jnp.bfloat16)).astype(jnp.float32)


def local(inputs, upstream, gates, routes, w_gate, w_up, w_down):
    experts = lax.axis_size("expert")
    fsdp_count = lax.axis_size("fsdp")
    tok_count = inputs.shape[0]
    route_count = routes.shape[1]
    capacity = min(tok_count, 3 * tok_count * route_count // experts)
    width = inputs.shape[1]
    sent_inputs, sent_scaled, token_table = dispatch(
        inputs, upstream, gates, routes, experts, capacity
    )
    got_inputs, got_scaled = (
        lax.all_to_all(
            sent_inputs.reshape(experts, capacity, width),
            "expert",
            split_axis=0,
            concat_axis=0,
            tiled=True,
        ),
        lax.all_to_all(
            sent_scaled.reshape(experts, capacity, width),
            "expert",
            split_axis=0,
            concat_axis=0,
            tiled=True,
        ),
    )
    row_count = experts * capacity
    rows_in = got_inputs.reshape(row_count, width)
    rows_scaled = got_scaled.reshape(row_count, width)
    own_gate = w_gate[0]
    own_up = w_up[0]
    own_down = w_down[0]
    block_h = own_gate.shape[0]
    total_h = block_h * fsdp_count
    empty_rows = jnp.zeros((row_count, width), jnp.float32)
    empty_grad = jnp.zeros((total_h, width), jnp.float32)
    pieces = (
        lax.all_gather(own_gate, "fsdp", axis=0, tiled=True),
        lax.all_gather(own_up, "fsdp", axis=0, tiled=True),
        lax.all_gather(own_down, "fsdp", axis=0, tiled=True),
    )
    d_input = empty_rows
    sum_gate = empty_grad
    sum_up = empty_grad
    sum_down = empty_grad
    for block_index in range(pieces[0].shape[0] // block_h):
        low_row = block_index * block_h
        term, grad_g, grad_u, grad_d = block_backward(
            rows_in,
            rows_scaled,
            pieces[0][low_row : low_row + block_h],
            pieces[1][low_row : low_row + block_h],
            pieces[2][low_row : low_row + block_h],
        )
        d_input = d_input + rounded(term)
        sum_gate = lax.dynamic_update_slice_in_dim(sum_gate, grad_g, low_row, 0)
        sum_up = lax.dynamic_update_slice_in_dim(sum_up, grad_u, low_row, 0)
        sum_down = lax.dynamic_update_slice_in_dim(sum_down, grad_d, low_row, 0)
    d_input, sum_gate, sum_up, sum_down = (d_input, sum_gate, sum_up, sum_down)
    shares = (
        lax.psum_scatter(
            sum_gate.astype(jnp.bfloat16), ("fsdp", "dp"), scatter_dimension=0, tiled=True
        ).astype(jnp.float32),
        lax.psum_scatter(
            sum_up.astype(jnp.bfloat16), ("fsdp", "dp"), scatter_dimension=0, tiled=True
        ).astype(jnp.float32),
        lax.psum_scatter(
            sum_down.astype(jnp.bfloat16), ("fsdp", "dp"), scatter_dimension=0, tiled=True
        ).astype(jnp.float32),
    )
    final_gate, final_up, final_down = (
        lax.all_gather(shares[0].astype(jnp.bfloat16), "dp", axis=0, tiled=True),
        lax.all_gather(shares[1].astype(jnp.bfloat16), "dp", axis=0, tiled=True),
        lax.all_gather(shares[2].astype(jnp.bfloat16), "dp", axis=0, tiled=True),
    )
    d_rows = d_input.astype(jnp.bfloat16).reshape(experts, capacity, width)
    returned = lax.all_to_all(d_rows, "expert", split_axis=0, concat_axis=0, tiled=True)
    contract_first = (((0,), (0,)), ((), ()))
    d_tokens = lax.dot_general(
        token_table,
        returned.reshape(experts * capacity, width),
        contract_first,
        preferred_element_type=jnp.float32,
    )
    return (d_tokens.astype(jnp.bfloat16), final_gate[None], final_up[None], final_down[None])


def solution(mesh):
    in_specs = (
        P(("expert", "fsdp", "dp"), None),
        P(("expert", "fsdp", "dp"), None),
        P(("expert", "fsdp", "dp"), None),
        P(("expert", "fsdp", "dp"), None),
        P("expert", "fsdp", None),
        P("expert", "fsdp", None),
        P("expert", "fsdp", None),
    )
    out_specs = (
        P(("expert", "fsdp", "dp"), None),
        P("expert", "fsdp", None),
        P("expert", "fsdp", None),
        P("expert", "fsdp", None),
    )
    return jax.shard_map(local, mesh=mesh, in_specs=in_specs, out_specs=out_specs, check_vma=False)
```

profile of v0, /device:TPU:1, one launch (start us, length us, event | category | flops | bytes accessed | tf_op | source)
XLA Modules:
  0.0 474.2 jit_solution(8872605721109293235)
XLA Ops:
  11.6 2.0 convolution_convert_fusion.1
  13.6 2.3 reshape.59
  15.9 7.3 %all-to-all-start = ((bf16[16,36,2048]{2,1,0:T(8,128)(2,1)}), bf16[16,36,2048]{2,1,0:T(8,128)(2,1)S(1)}, u32[]{:S(2)}, u32[]{:S(2)}) async-start(bf16[16,36,2048]{2,1,0:T(8,128)(2,1)} %reshape.59), calls=%async_computation | async-start | bytes 5242880 | tf_op jit(solution)/shard_map/all_to_all | solution.py:81
  24.0 2.2 convolution_convert_fusion
  26.2 4.1 reshape.61
  30.4 25.5 %all-to-all-done = bf16[16,36,2048]{2,1,0:T(8,128)(2,1)S(1)} async-done(((bf16[16,36,2048]{2,1,0:T(8,128)(2,1)}), bf16[16,36,2048]{2,1,0:T(8,128)(2,1)S(1)}, u32[]{:S(2)}, u32[]{:S(2)}) %all-to-all-start) | async-done | bytes 2359328 | tf_op jit(solution)/shard_map/all_to_all | solution.py:81
  55.9 5.1 %all-to-all-start.1 = ((bf16[16,36,2048]{2,1,0:T(8,128)(2,1)}), bf16[16,36,2048]{2,1,0:T(8,128)(2,1)}, u32[]{:S(2)}, u32[]{:S(2)}) async-start(bf16[16,36,2048]{2,1,0:T(8,128)(2,1)} %reshape.61), calls=%async_computation.1 | async-start | bytes 5242880 | tf_op jit(solution)/shard_map/all_to_all | solution.py:74
  61.9 2.2 reshape.60
  64.1 29.8 %all-to-all-done.1 = bf16[16,36,2048]{2,1,0:T(8,128)(2,1)} async-done(((bf16[16,36,2048]{2,1,0:T(8,128)(2,1)}), bf16[16,36,2048]{2,1,0:T(8,128)(2,1)}, u32[]{:S(2)}, u32[]{:S(2)}) %all-to-all-start.1) | async-done | bytes 2359328 | tf_op jit(solution)/shard_map/all_to_all | solution.py:74
  93.9 2.7 reshape.62
  96.6 2.1 fusion.6
  99.9 2.9 fusion.4
  102.9 41.2 %all-gather.7.cloned.1.call-done = bf16[1,768,2048]{2,1,0:T(8,128)(2,1)} async-done(((bf16[1,192,2048]{2,1,0:T(8,128)(2,1)}), bf16[1,768,2048]{2,1,0:T(8,128)(2,1)}) %all-gather.7.cloned.1.call-update) | async-done | bytes 3145744 | tf_op jit(solution)/shard_map/all_gather | solution.py:102
  144.1 3.0 multiply_convert_fusion.10
  148.7 2.1 dynamic_update_slice.36
  165.5 1.8 multiply_convert_fusion.4
  170.6 2.0 dynamic_update_slice.40
  179.3 1.8 fusion.20
  185.1 2.2 add_convert_fusion.1
  188.3 2.3 add_convert_fusion.2
  191.5 2.3 add_convert_fusion.3
  198.7 2.1 fusion.5
  200.9 2.1 add_convert_fusion.4
  204.3 3.5 add_convert_fusion
  207.8 2.6 reshape.63
  210.4 49.6 %all_to_all.15 = bf16[16,36,2048]{2,1,0:T(8,128)(2,1)} all-to-all(bf16[16,36,2048]{2,1,0:T(8,128)(2,1)S(1)} %reshape.63), channel_id=1, replica_groups=mesh['expert'=16,'fsdp'=4,'dp'=4] {'expert'}, dimensions={0} | all-to-all | bytes 4718592 | tf_op jit(solution)/shard_map/all_to_all | solution.py:139
  260.0 2.7 reshape.64
  264.0 19.7 %all_gather.21 = bf16[192,2048]{1,0:T(8,128)(2,1)S(1)} all-gather(bf16[48,2048]{1,0:T(8,128)(2,1)} %reduce-scatter.4.cloned.1.call-done), channel_id=1, replica_groups=mesh['expert'=16,'fsdp'=4,'dp'=4] {'dp'}, dimensions={0}, use_global_device_ids=true | all-gather | bytes 983040 | tf_op jit(solution)/shard_map/all_gather | solution.py:134
  283.7 71.8 %reduce-scatter.6.cloned.1.call-done = bf16[48,2048]{1,0:T(8,128)(2,1)} async-done(((bf16[768,2048]{1,0:T(8,128)(2,1)}), bf16[48,2048]{1,0:T(8,128)(2,1)}) %reduce-scatter.6.cloned.1.call-update) | async-done | bytes 196624 | tf_op jit(solution)/shard_map/reduce_scatter | solution.py:126
  355.5 15.4 %all_gather.22 = bf16[192,2048]{1,0:T(8,128)(2,1)S(1)} all-gather(bf16[48,2048]{1,0:T(8,128)(2,1)} %reduce-scatter.6.cloned.1.call-done), channel_id=1, replica_groups=mesh['expert'=16,'fsdp'=4,'dp'=4] {'dp'}, dimensions={0}, use_global_device_ids=true | all-gather | bytes 983040 | tf_op jit(solution)/shard_map/all_gather | solution.py:135
  370.9 78.0 %reduce-scatter.8.cloned.1.call-done = bf16[48,2048]{1,0:T(8,128)(2,1)} async-done(((bf16[768,2048]{1,0:T(8,128)(2,1)}), bf16[48,2048]{1,0:T(8,128)(2,1)}) %reduce-scatter.8.cloned.1.call-update) | async-done | bytes 196624 | tf_op jit(solution)/shard_map/reduce_scatter | solution.py:129
  448.9 15.9 %all_gather.23 = bf16[192,2048]{1,0:T(8,128)(2,1)S(1)} all-gather(bf16[48,2048]{1,0:T(8,128)(2,1)} %reduce-scatter.8.cloned.1.call-done), channel_id=1, replica_groups=mesh['expert'=16,'fsdp'=4,'dp'=4] {'dp'}, dimensions={0}, use_global_device_ids=true | all-gather | bytes 983040 | tf_op jit(solution)/shard_map/all_gather | solution.py:136
  (145 shorter events, 49.2 us)
Async XLA Ops:
  7.2 4.4 copy-start
  7.2 89.4 %all-gather.11.cloned.1.call-start = ((), (), s32[]{:S(2)}) async-start(), calls=%async_computation.11 | async-start | bytes 3932160 | tf_op jit(solution)/shard_map/all_gather | solution.py:100
  15.9 8.2 %copy-start.28 = (bf16[96,2048]{1,0:T(8,128)(2,1)S(1)}, bf16[96,2048]{1,0:T(8,128)(2,1)}, u32[]{:S(2)}) copy-start(bf16[96,2048]{1,0:T(8,128)(2,1)} %param.7) | copy-start | bytes 1179652
  15.9 40.0 %all-to-all-start = ((bf16[16,36,2048]{2,1,0:T(8,128)(2,1)}), bf16[16,36,2048]{2,1,0:T(8,128)(2,1)S(1)}, u32[]{:S(2)}, u32[]{:S(2)}) async-start(bf16[16,36,2048]{2,1,0:T(8,128)(2,1)} %reshape.59), calls=%async_computation | async-start | bytes 5242880 | tf_op jit(solution)/shard_map/all_to_all | solution.py:81
  23.2 76.8 %all-gather.9.cloned.1.call-start = ((), (), s32[]{:S(2)}) async-start(), calls=%async_computation.10 | async-start | bytes 3932160 | tf_op jit(solution)/shard_map/all_gather | solution.py:101
  55.9 38.0 %all-to-all-start.1 = ((bf16[16,36,2048]{2,1,0:T(8,128)(2,1)}), bf16[16,36,2048]{2,1,0:T(8,128)(2,1)}, u32[]{:S(2)}, u32[]{:S(2)}) async-start(bf16[16,36,2048]{2,1,0:T(8,128)(2,1)} %reshape.61), calls=%async_computation.1 | async-start | bytes 5242880 | tf_op jit(solution)/shard_map/all_to_all | solution.py:74
  61.0 83.2 %all-gather.7.cloned.1.call-start = ((), (), s32[]{:S(2)}) async-start(), calls=%async_computation.9 | async-start | bytes 3932160 | tf_op jit(solution)/shard_map/all_gather | solution.py:102
  61.7 202.3 %reduce-scatter.4.cloned.1.call-start = ((), (), s32[]{:S(2)}) async-start(), calls=%async_computation.6 | async-start | bytes 3342336 | tf_op jit(solution)/shard_map/reduce_scatter | solution.py:123
  98.7 48.4 %copy-start.42 = (f32[576,192]{0,1:T(8,128)}, f32[576,192]{0,1:T(8,128)S(1)}, u32[]{:S(2)}) copy-start(f32[576,192]{0,1:T(8,128)S(1)} %fusion.6) | copy-start | bytes 1327108
  147.2 22.6 %copy-start.20 = (bf16[576,192]{0,1:T(8,128)(2,1)}, bf16[576,192]{0,1:T(8,128)(2,1)S(1)}, u32[]{:S(2)}) copy-start(bf16[576,192]{0,1:T(8,128)(2,1)S(1)} %get-tuple-element.4) | copy-start | bytes 663556
  148.7 3.0 copy-start.6
  151.7 2.9 copy-start.29
  153.6 3.2 copy-start.30
  153.6 2.1 copy-start.10
  156.8 2.7 copy-start.14
  156.8 15.9 %copy-start.22 = (bf16[576,192]{0,1:T(8,128)(2,1)}, bf16[576,192]{0,1:T(8,128)(2,1)S(1)}, u32[]{:S(2)}) copy-start(bf16[576,192]{0,1:T(8,128)(2,1)S(1)} %get-tuple-element.6) | copy-start | bytes 663556
  159.5 2.2 copy-start.34
  161.7 2.7 copy-start.16
  161.7 12.6 %copy-start.24 = (bf16[576,192]{0,1:T(8,128)(2,1)}, bf16[576,192]{0,1:T(8,128)(2,1)S(1)}, u32[]{:S(2)}) copy-start(bf16[576,192]{0,1:T(8,128)(2,1)S(1)} %get-tuple-element.8) | copy-start | bytes 663556
  164.4 2.8 copy-start.38
  169.7 185.8 %reduce-scatter.6.cloned.1.call-start = ((), (), s32[]{:S(2)}) async-start(), calls=%async_computation.7 | async-start | bytes 3342336 | tf_op jit(solution)/shard_map/reduce_scatter | solution.py:126
  177.7 271.2 %reduce-scatter.8.cloned.1.call-start = ((), (), s32[]{:S(2)}) async-start(), calls=%async_computation.8 | async-start | bytes 3342336 | tf_op jit(solution)/shard_map/reduce_scatter | solution.py:129
  185.1 2.2 copy-start.17
  188.3 2.3 copy-start.15
  191.5 2.3 copy-start.12
  191.5 2.3 copy-start.31
  191.5 2.3 copy-start.33
  198.7 2.1 copy-start.21
  200.9 2.2 copy-start.3
  200.9 2.7 copy-start.4
  200.9 3.4 copy-start.5
  370.9 96.5 %copy-start.1 = (bf16[96,2048]{1,0:T(8,128)(2,1)S(1)}, bf16[96,2048]{1,0:T(8,128)(2,1)}, u32[]{:S(2)}) copy-start(bf16[96,2048]{1,0:T(8,128)(2,1)} %param.8) | copy-start | bytes 1179652
  (20 other events, 28.5 us)
Sparse Core Ops, SparseCore 0:
  9.8 45.9 all-gather.10
  57.6 42.3 all-gather.8
  101.8 42.3 all-gather.6
  169.9 93.3 reduce-scatter.3
  266.7 88.7 reduce-scatter.5
  359.0 89.8 reduce-scatter.7
where the time goes:
time: 479 us; the launch traced here: 474 us
  waiting for transfers between devices  250 us (52%)
  blocking collectives  101 us (21%)
  matrix products  53.2 us (11%)
  local copies, waits for them, and re-layouts  37.2 us (8%)
  between operations  14.6 us (3%)
  starting transfers between devices  13 us (3%)
  other arithmetic  5.95 us (1%)
    reduce_scatter x1, waiting for transfers between devices, local(): lax.psum_scatter(sum_down.astype(jnp.bfloat16), ('fsdp', 'dp'), scatter_d...  78 us
    reduce_scatter x1, waiting for transfers between devices, local(): lax.psum_scatter(sum_up.astype(jnp.bfloat16), ('fsdp', 'dp'), scatter_dim...  71.8 us
    all_to_all x1, blocking collectives, local(): lax.all_to_all(d_rows, 'expert', split_axis=0, concat_axis=0, tiled=True)  49.6 us
    all_gather x1, waiting for transfers between devices, local(): lax.all_gather(own_down, 'fsdp', axis=0, tiled=True)  41.2 us
    all_to_all x1, waiting for transfers between devices, local(): lax.all_to_all(sent_inputs.reshape(experts, capacity, width), 'expert', s...  29.8 us
    all_to_all x1, waiting for transfers between devices, local(): lax.all_to_all(sent_scaled.reshape(experts, capacity, width), 'expert', s...  25.5 us
    all_gather x1, blocking collectives, local(): lax.all_gather(shares[0].astype(jnp.bfloat16), 'dp', axis=0, tiled=True)  19.7 us
    all_gather x1, blocking collectives, local(): lax.all_gather(shares[2].astype(jnp.bfloat16), 'dp', axis=0, tiled=True)  15.9 us
  transfers between devices with their start and end apart: 8, of which 6 were waited for; matrix products, arithmetic and copies ran while one was open for 13% of the time, Pallas kernels for 0%

commit v1 on v0

v1 whole, which is shorter than its diff:
```python
import functools

import jax
import jax.numpy as jnp
from jax import lax
from jax.experimental import pallas as pl
from jax.experimental.pallas import tpu as pltpu
from jax.sharding import PartitionSpec as P

MESH_ID = pl.DeviceIdType.MESH
F32 = jnp.float32
BF16 = jnp.bfloat16

TOK = 96
CAP = 36
D = 2048
BLK = 192
XN = 4
GN = 4
FN = 4
DN = 4
GT = GN * TOK
CHUNK = GN * CAP
ROWS = XN * CHUNK
HALF = 2 * BLK
QUART = BLK // DN
NC = 2
CW = D // NC

NSEM = 128


def dot_nt(a, b):
    return lax.dot_general(a, b, (((1,), (1,)), ((), ())), preferred_element_type=F32)


def dot_nn(a, b):
    return lax.dot_general(a, b, (((1,), (0,)), ((), ())), preferred_element_type=F32)


def dot_tn(a, b):
    return lax.dot_general(a, b, (((0,), (0,)), ((), ())), preferred_element_type=F32)


def kernel(
    meta_ref, x_ref, u_ref, wg_ref, wu_ref, wd_ref,
    out_x, out_g, out_u, out_d,
    metas, tok, tab, gsl, snd, rows, wts, gu, dh, dgu, tr, gacc, gsend, grecv,
    red_a, red_b, red_p, red_n, fin, p_own, p_send, p_recv, q, part, core_recv,
    z_send, z_recv, gout, ssem, rsem, lsem,
):
    e = lax.axis_index("expert")
    f = lax.axis_index("fsdp")
    d = lax.axis_index("dp")
    core = lax.rem(e, 2)
    sib_e = e + 1 - 2 * core
    zp_e = e + 2 - 4 * lax.rem(lax.div(e, 2), 2)
    diag_e = zp_e + 1 - 2 * core
    near = f + 1 - 2 * lax.rem(f, 2)
    far = FN - 1 - f
    row_f = near + core * (far - near)
    wgt_f = far + core * (near - far)
    up_d = lax.rem(d + 1, DN)
    dn_d = lax.rem(d + DN - 1, DN)
    op_d = lax.rem(d + 2, DN)

    sib = {"expert": sib_e}
    zp = {"expert": zp_e}
    diag = {"expert": diag_e}
    x_at = [{"expert": lax.rem(e + GN * o, XN * GN)} for o in range(XN)]
    row_y = {"fsdp": row_f}
    wgt_y = {"fsdp": wgt_f}
    d_up = {"dp": up_d}
    d_dn = {"dp": dn_d}

    used = [0]

    def remote(src, dst, dev):
        i = used[0]
        used[0] += 1
        return pltpu.make_async_remote_copy(
            src_ref=src, dst_ref=dst, send_sem=ssem.at[i], recv_sem=rsem.at[i],
            device_id=dev, device_id_type=MESH_ID,
        )

    pending = {}

    def send(src, dst, dev):
        c = remote(src, dst, dev)
        c.start()
        pending[id(c)] = c
        return c

    lused = [0]

    def local_copy(src, dst):
        i = lused[0]
        lused[0] += 1
        c = pltpu.make_async_copy(src, dst, lsem.at[i])
        c.start()
        return c

    toks = (x_ref, u_ref)
    own_tok = [local_copy(toks[a], tok.at[a, pl.ds(0, TOK)]) for a in range(2)]
    weights = (wg_ref, wu_ref, wd_ref)
    own_wts = [local_copy(weights[m], wts.at[pl.ds(m * HALF, BLK)]) for m in range(3)]

    partners = [sib, zp, diag] + x_at[1:] + [row_y, wgt_y, d_up, d_dn]
    barrier = pltpu.get_barrier_semaphore()
    for dev in partners:
        pl.semaphore_signal(barrier, inc=1, device_id=dev, device_id_type=MESH_ID)
    pl.semaphore_wait(barrier, len(partners))

    meta_c = [send(meta_ref, metas.at[i], dev) for i, dev in enumerate((zp, sib, diag))]
    tok_z = {}
    tok_s = {}
    for a in range(2):
        for c in range(NC):
            cols = pl.ds(c * CW, CW)
            tok_z[a, c] = send(toks[a].at[:, cols], tok.at[a, pl.ds(TOK, TOK), cols], zp)
            tok_s[a, c] = send(toks[a].at[:, cols], tok.at[a, pl.ds(2 * TOK, TOK), cols], sib)
    wts_c = [
        send(weights[m], wts.at[pl.ds(m * HALF + BLK, BLK)], wgt_y) for m in range(3)
    ]

    for c in meta_c:
        c.wait_recv()
    lane = lax.broadcasted_iota(jnp.int32, (8, GT), 1)
    meta = meta_ref[...]
    for r in range(1, GN):
        meta = jnp.where(lane >= r * TOK, metas[r - 1], meta)
    source = sum((lane >= r * TOK).astype(F32) for r in range(1, GN))
    relative = lax.broadcasted_iota(jnp.int32, (8, GT), 0)
    expert = lax.rem(e + GN * relative, XN * GN).astype(F32)
    hit0 = meta[0:1] == expert
    hit1 = meta[1:2] == expert
    hit = jnp.logical_or(hit0, hit1)
    t_row = lax.broadcasted_iota(jnp.int32, (GT, GT), 0)
    t_col = lax.broadcasted_iota(jnp.int32, (GT, GT), 1)
    first = sum(jnp.where(t_col >= r * TOK, TOK, 0) for r in range(1, GN))
    before = jnp.logical_and(t_row < t_col, t_row >= first)
    earlier = dot_nn(
        jnp.where(hit, 1.0, 0.0).astype(BF16), jnp.where(before, 1.0, 0.0).astype(BF16)
    )
    target = jnp.where(hit, source * CAP + earlier, -1.0)
    weight = jnp.where(hit0, meta[2:3], jnp.where(hit1, meta[3:4], 0.0))
    slot = lax.broadcasted_iota(jnp.int32, (CHUNK, GT), 0).astype(F32)
    for o in range(XN):
        same = slot == target[o : o + 1]
        at = pl.ds(o * CHUNK, CHUNK)
        tab[at, :] = jnp.where(same, 1.0, 0.0).astype(BF16)
        gates = jnp.sum(jnp.where(same, weight[o : o + 1], 0.0), axis=1, keepdims=True)
        gsl[at, :] = jnp.broadcast_to(gates, (CHUNK, 128))

    x_c = {}
    y_c = {}

    def to_row_partner(a, c, k):
        cols = pl.ds(c * CW, CW)
        y_c[a, c, k] = send(
            rows.at[a, pl.ds(k * CHUNK, CHUNK), cols],
            rows.at[a, pl.ds(ROWS + k * CHUNK, CHUNK), cols],
            row_y,
        )

    for a in range(2):
        own_tok[a].wait()
        for c in range(NC):
            cols = pl.ds(c * CW, CW)
            tok_z[a, c].wait_recv()
            fwd = send(
                tok.at[a, pl.ds(TOK, TOK), cols], tok.at[a, pl.ds(3 * TOK, TOK), cols], sib
            )
            tok_s[a, c].wait_recv()
            fwd.wait_recv()

            @pl.loop(0, CW // 512)
            def _(n):
                tile = pl.ds(pl.multiple_of(c * CW + n * 512, 512), 512)
                picked = dot_nn(tab[...], tok[a, :, tile])
                if a == 1:
                    picked = picked * gsl[:, 0:1]
                picked = picked.astype(BF16)
                rows[a, pl.ds(0, CHUNK), tile] = picked[0:CHUNK]
                for o in range(1, XN):
                    snd[a, o - 1, :, tile] = picked[o * CHUNK : (o + 1) * CHUNK]

            for o in (2, 1, 3):
                slot_at = (XN - o) % XN
                x_c[a, c, o] = send(
                    snd.at[a, o - 1, :, cols],
                    rows.at[a, pl.ds(slot_at * CHUNK, CHUNK), cols],
                    x_at[o],
                )
            to_row_partner(a, c, 0)

    def pass_on(a, c):
        for o in (1, 3, 2):
            x_c[a, c, o].wait_recv()
            to_row_partner(a, c, (XN - o) % XN)

    def gate_up(s):
        at = pl.ds(s * ROWS, ROWS)

        @pl.loop(0, 3)
        def _(n):
            tile = pl.ds(pl.multiple_of(n * 256, 256), 256)
            gu[at, tile] = dot_nt(rows[0, at, :], wts[tile, :])

    def d_hidden(s):
        at = pl.ds(s * ROWS, ROWS)
        dh[at, :] = dot_nt(rows[1, at, :], wts[pl.ds(2 * HALF, HALF), :])

    def elementwise(low, high):
        @pl.loop(low, high)
        def _(i):
            at = pl.ds(pl.multiple_of(i * 128, 128), 128)
            gate = gu[at, pl.ds(0, HALF)]
            upward = gu[at, pl.ds(HALF, HALF)]
            dhid = dh[at, :]
            logistic = jax.nn.sigmoid(gate)
            active = gate * logistic
            slope = logistic * (1.0 + gate * (1.0 - logistic))
            hidden = (active * upward).astype(BF16)
            d_up_ = (dhid * active).astype(BF16)
            d_gate = (dhid * upward * slope).astype(BF16)
            dgu[at, pl.ds(0, HALF)] = d_gate
            dgu[at, pl.ds(HALF, HALF)] = d_up_
            for m, value in enumerate((d_gate, d_up_, hidden)):
                turned = value.T
                tr[pl.ds(m * BLK, BLK), at] = turned[BLK:HALF]
                tr[pl.ds((3 + m) * BLK, BLK), at] = turned[0:BLK]

    for c in range(NC):
        pass_on(0, c)
    for c in own_wts:
        c.wait()
    for c in wts_c:
        c.wait_recv()
    gate_up(0)
    pass_on(1, 0)
    for c in range(NC):
        for k in range(XN):
            y_c[0, c, k].wait_recv()
    gate_up(1)
    for c in range(1, NC):
        pass_on(1, c)
    d_hidden(0)
    elementwise(0, ROWS // 128)
    for c in range(NC):
        for k in range(XN):
            y_c[1, c, k].wait_recv()
    d_hidden(1)
    elementwise(ROWS // 128, 2 * ROWS // 128)

    @pl.loop(0, D // 512)
    def _(n):
        tile = pl.ds(pl.multiple_of(n * 512, 512), 512)
        value = dot_nn(tr[pl.ds(0, 2 * BLK), :], rows[0, :, tile]).astype(BF16)
        gsend[0, :, tile] = value[0:BLK]
        gsend[1, :, tile] = value[BLK : 2 * BLK]

    g_c = [send(gsend.at[m], grecv.at[m], wgt_y) for m in range(2)]

    @pl.loop(0, D // 512)
    def _(n):
        tile = pl.ds(pl.multiple_of(n * 512, 512), 512)
        gsend[2, :, tile] = dot_nn(tr[pl.ds(2 * BLK, BLK), :], rows[1, :, tile]).astype(BF16)

    g_c.append(send(gsend.at[2], grecv.at[2], wgt_y))

    p_c = []
    for c in range(NC):

        @pl.loop(0, CW // 512)
        def _(n):
            tile = pl.ds(pl.multiple_of(c * CW + n * 512, 512), 512)
            p_send[:, tile] = dot_nn(
                dgu[pl.ds(ROWS, ROWS), :], wts[pl.ds(0, 2 * HALF), tile]
            ).astype(BF16)

        cols = pl.ds(c * CW, CW)
        p_c.append(send(p_send.at[:, cols], p_recv.at[:, cols], row_y))

    @pl.loop(0, D // 512)
    def _(n):
        tile = pl.ds(pl.multiple_of(n * 512, 512), 512)
        value = dot_nn(tr[pl.ds(3 * BLK, 2 * BLK), :], rows[0, :, tile])
        gacc[0, :, tile] = value[0:BLK]
        gacc[1, :, tile] = value[BLK : 2 * BLK]
        gacc[2, :, tile] = dot_nn(tr[pl.ds(5 * BLK, BLK), :], rows[1, :, tile])

    lo = pl.ds(0, D // 2)
    hi = pl.ds(D // 2, D // 2)

    def quarter(i):
        return pl.ds(pl.multiple_of(i * QUART, QUART), QUART)

    r1 = {}
    r2 = {}
    a1 = {}
    a2 = {}

    def reduce_first(m):
        g_c[m].wait_recv()
        g_c[m].wait_send()
        del pending[id(g_c[m])]

        @pl.loop(0, BLK // 16)
        def _(i):
            at = pl.ds(pl.multiple_of(i * 16, 16), 16)
            gsend[m, at, :] = (gacc[m, at, :] + grecv[m, at, :].astype(F32)).astype(BF16)

        r1[m] = (
            send(gsend.at[m, quarter(op_d), lo], red_a.at[m], d_up),
            send(gsend.at[m, quarter(op_d), hi], red_b.at[m], d_dn),
        )

    def reduce_second(m):
        r1[m][0].wait_recv()
        at = quarter(up_d)
        gsend[m, at, lo] = (gsend[m, at, lo].astype(F32) + red_a[m].astype(F32)).astype(BF16)
        first_c = send(gsend.at[m, at, :], red_p.at[m], d_up)
        r1[m][1].wait_recv()
        at = quarter(dn_d)
        gsend[m, at, hi] = (gsend[m, at, hi].astype(F32) + red_b[m].astype(F32)).astype(BF16)
        r2[m] = (first_c, send(gsend.at[m, at, :], red_n.at[m], d_dn))

    def gather_first(m):
        r2[m][0].wait_recv()
        r2[m][1].wait_recv()
        at = quarter(d)
        fin[m, at, :] = (
            gsend[m, at, :].astype(F32) + red_p[m].astype(F32) + red_n[m].astype(F32)
        ).astype(BF16)
        a1[m] = (
            send(fin.at[m, at, :], fin.at[m, at, :], d_up),
            send(fin.at[m, at, :], fin.at[m, at, :], d_dn),
        )

    def gather_second(m):
        a1[m][0].wait_recv()
        at = quarter(dn_d)
        first_c = send(fin.at[m, at, lo], fin.at[m, at, lo], d_up)
        a1[m][1].wait_recv()
        at = quarter(up_d)
        a2[m] = (first_c, send(fin.at[m, at, hi], fin.at[m, at, hi], d_dn))

    outs = (out_g, out_u, out_d)
    done = []

    def finish(m):
        a2[m][0].wait_recv()
        a2[m][1].wait_recv()
        done.append(local_copy(fin.at[m], outs[m]))

    q_c = {}
    s_c = {}
    z_c = {}

    def return_rows(c):
        cols = pl.ds(c * CW, CW)
        p_c[c].wait_recv()
        p_c[c].wait_send()
        del pending[id(p_c[c])]

        @pl.loop(0, ROWS // 48)
        def _(i):
            at = pl.ds(pl.multiple_of(i * 48, 48), 48)
            p_send[at, cols] = (p_own[at, cols] + p_recv[at, cols].astype(F32)).astype(BF16)

        for k in (2, 1, 3):
            q_c[c, k] = send(
                p_send.at[pl.ds(k * CHUNK, CHUNK), cols],
                q.at[pl.ds((XN - k) % XN * CHUNK, CHUNK), cols],
                x_at[k],
            )
        q[pl.ds(0, CHUNK), cols] = p_send[pl.ds(0, CHUNK), cols]

    def combine(c):
        cols = pl.ds(c * CW, CW)
        for k in (1, 3, 2):
            q_c[c, k].wait_recv()

        @pl.loop(0, CW // 512)
        def _(n):
            tile = pl.ds(pl.multiple_of(c * CW + n * 512, 512), 512)
            part[:, tile] = dot_tn(tab[...], q[:, tile]).astype(BF16)

        s_c[c] = send(part.at[pl.ds(2 * TOK, 2 * TOK), cols], core_recv.at[:, cols], sib)

    def along_z(c):
        cols = pl.ds(c * CW, CW)
        s_c[c].wait_recv()
        z_send[:, cols] = (
            part[pl.ds(TOK, TOK), cols].astype(F32)
            + core_recv[pl.ds(TOK, TOK), cols].astype(F32)
        ).astype(BF16)
        z_c[c] = send(z_send.at[:, cols], z_recv.at[:, cols], zp)

    def tokens_out(c):
        cols = pl.ds(c * CW, CW)
        z_c[c].wait_recv()
        gout[:, cols] = (
            part[pl.ds(0, TOK), cols].astype(F32)
            + core_recv[pl.ds(0, TOK), cols].astype(F32)
            + z_recv[:, cols].astype(F32)
        ).astype(BF16)
        done.append(local_copy(gout.at[:, cols], out_x.at[:, cols]))

    reduce_first(0)

    @pl.loop(0, D // 512)
    def _(n):
        tile = pl.ds(pl.multiple_of(n * 512, 512), 512)
        p_own[:, tile] = dot_nn(dgu[pl.ds(0, ROWS), :], wts[pl.ds(0, 2 * HALF), tile])

    reduce_first(1)
    reduce_second(0)
    reduce_first(2)
    reduce_second(1)
    gather_first(0)
    return_rows(0)
    reduce_second(2)
    gather_second(0)
    gather_first(1)
    return_rows(1)
    gather_first(2)
    gather_second(1)
    finish(0)
    combine(0)
    along_z(0)
    gather_second(2)
    finish(1)
    combine(1)
    along_z(1)
    tokens_out(0)
    tokens_out(1)
    finish(2)
    for c in done:
        c.wait()
    for c in pending.values():
        c.wait_send()


SCRATCH = (
    ((GN - 1, 8, GT), F32),
    ((2, GT, D), BF16),
    ((ROWS, GT), BF16),
    ((ROWS, 128), F32),
    ((2, XN - 1, CHUNK, D), BF16),
    ((2, 2 * ROWS, D), BF16),
    ((3 * HALF, D), BF16),
    ((2 * ROWS, 2 * HALF), F32),
    ((2 * ROWS, HALF), F32),
    ((2 * ROWS, 2 * HALF), BF16),
    ((6 * BLK, 2 * ROWS), BF16),
    ((3, BLK, D), F32),
    ((3, BLK, D), BF16),
    ((3, BLK, D), BF16),
    ((3, QUART, D // 2), BF16),
    ((3, QUART, D // 2), BF16),
    ((3, QUART, D), BF16),
    ((3, QUART, D), BF16),
    ((3, BLK, D), BF16),
    ((ROWS, D), F32),
    ((ROWS, D), BF16),
    ((ROWS, D), BF16),
    ((ROWS, D), BF16),
    ((GT, D), BF16),
    ((2 * TOK, D), BF16),
    ((TOK, D), BF16),
    ((TOK, D), BF16),
    ((TOK, D), BF16),
)


def local(inputs, upstream, gates, routes, w_gate, w_up, w_down):
    meta = jnp.concatenate(
        [routes.T.astype(F32), gates.T, jnp.zeros((4, TOK), F32)], axis=0
    )
    meta = jnp.tile(meta, (1, GN))
    anywhere = pl.BlockSpec(memory_space=pl.ANY)
    outs = pl.pallas_call(
        kernel,
        out_shape=(
            jax.ShapeDtypeStruct((TOK, D), BF16),
            jax.ShapeDtypeStruct((BLK, D), BF16),
            jax.ShapeDtypeStruct((BLK, D), BF16),
            jax.ShapeDtypeStruct((BLK, D), BF16),
        ),
        in_specs=[pl.BlockSpec(memory_space=pltpu.VMEM)] + [anywhere] * 5,
        out_specs=[anywhere] * 4,
        scratch_shapes=[pltpu.VMEM(shape, dtype) for shape, dtype in SCRATCH]
        + [
            pltpu.SemaphoreType.DMA((NSEM,)),
            pltpu.SemaphoreType.DMA((NSEM,)),
            pltpu.SemaphoreType.DMA((16,)),
        ],
        compiler_params=pltpu.CompilerParams(
            collective_id=0, has_side_effects=True, vmem_limit_bytes=62 * 2**20
        ),
        name="expert_backward",
    )(meta, inputs, upstream, w_gate[0], w_up[0], w_down[0])
    return outs[0], outs[1][None], outs[2][None], outs[3][None]


def solution(mesh):
    tokens = P(("expert", "fsdp", "dp"), None)
    hidden = P("expert", "fsdp", None)
    return jax.shard_map(
        local,
        mesh=mesh,
        in_specs=(tokens, tokens, tokens, tokens, hidden, hidden, hidden),
        out_specs=(tokens, hidden, hidden, hidden),
        check_vma=False,
    )
```

time: 479 us -> 226 us (0.47)
  waiting for transfers between devices: 250 us -> 0 us
  Pallas kernels: 0 us -> 217 us
  blocking collectives: 101 us -> 0 us
  matrix products: 53.2 us -> 0 us
  local copies, waits for them, and re-layouts: 37.2 us -> 7.6 us
  between operations: 14.6 us -> 0.67 us
  starting transfers between devices: 13 us -> 0 us
  other arithmetic: 5.95 us -> 0.07 us
    pallas_call x0 -> x1, Pallas kernels: none -> 217 us  [local(): pl.pallas_call(kernel, out_shape=(jax.ShapeDtypeStruct((TOK, D), BF16), j...]
    reduce_scatter x3 -> x0, waiting for transfers between devices: 150 us -> none  [the longest x1 78 us: local(): lax.psum_scatter(sum_down.astype(jnp.bfloat16), ('fsdp', 'dp'), scatter_d...]
    all_to_all x2 -> x0, waiting for transfers between devices: 55.3 us -> none  [the longest x1 29.8 us: local(): lax.all_to_all(sent_inputs.reshape(experts, capacity, width), 'expert', s...]
    dot_general x35 -> x0, matrix products: 53.2 us -> none  [the longest x4 8.91 us: block_backward(): jnp.dot(d_up, up_block, preferred_element_type=jnp.float32)]
    all_gather x3 -> x0, blocking collectives: 51 us -> none  [the longest x1 19.7 us: local(): lax.all_gather(shares[0].astype(jnp.bfloat16), 'dp', axis=0, tiled=True)]
    all_to_all x1 -> x0, blocking collectives: 49.6 us -> none  [local(): lax.all_to_all(d_rows, 'expert', split_axis=0, concat_axis=0, tiled=True)]
    all_gather x3 -> x0, waiting for transfers between devices: 42.5 us -> none  [the longest x1 41.2 us: local(): lax.all_gather(own_down, 'fsdp', axis=0, tiled=True)]
    reshape x6 -> x0, local copies, waits for them, and re-layouts: 16.5 us -> none  [the longest x1 4.12 us: local(): sent_inputs.reshape(experts, capacity, width)]
  transfers between devices with their start and end apart: 8 -> 0, of which waited for: 6 -> 0; matrix products, arithmetic and copies ran while one was open for 13% -> 0% of each run, Pallas kernels for 0% -> 0%
where the time goes in v1:
time: 226 us; the launch traced here: 225 us
  Pallas kernels  217 us (96%)
  local copies, waits for them, and re-layouts  7.6 us (3%)
    pallas_call x1, Pallas kernels, local(): pl.pallas_call(kernel, out_shape=(jax.ShapeDtypeStruct((TOK, D), BF16), j...  217 us
    unnamed x14, local copies, waits for them, and re-layouts  6.83 us

profile of v1, /device:TPU:1, one launch (start us, length us, event | category | flops | bytes accessed | tf_op | source)
XLA Modules:
  0.0 225.4 jit_solution(6300910260124534464)
XLA Ops:
  0.6 0.0 copy-start.3
  0.7 0.1 pad.2.clone
  0.7 0.6 copy-done.3
  1.3 0.0 copy-start.4
  1.3 0.7 copy-done.4
  2.0 0.1 maximum_maximum_fusion
  2.1 0.7 tile.10.meta_ref
  2.8 217.1 %expert_backward.1 = (bf16[96,2048]{1,0:T(8,128)(2,1)}, bf16[192,2048]{1,0:T(8,128)(2,1)}, bf16[192,2048]{1,0:T(8,128)(2,1)}, bf16[192,2048]{1,0:T(8,128)(2,1)}) custom-call(f32[8,384]{1,0:T(8,128)} %tile.10.meta_ref, bf16[96,2048]{1,0:T(8,128)(2,1)} %x_ref.1, bf16[96,2048]{1,0:T(8,128)(2,1)} %u_ref.1, bf16[192,2048]{1,0:T(8,128)(2,1)} %bitcast.12, ...), custom_call_target="tpu_custom_call" | custom-call | tf_op jit(solution)/shard_map/expert_backward/pallas_call | solution.py:484
  219.8 0.0 copy-start.2
  219.8 1.8 copy.15
  221.7 0.0 copy-done.2
  221.7 0.0 copy-start.1
  221.7 0.9 copy.16
  222.6 0.5 copy-done.1
  223.1 0.0 copy-start
  223.1 0.9 copy.17
  224.0 0.5 copy-done
  224.5 0.9 copy.18
  (3 shorter events, 0.0 us)
Async XLA Ops:
  0.6 0.7 copy-start.3
  1.3 0.7 copy-start.4
  219.8 1.9 copy-start.2
  221.7 1.4 copy-start.1
  223.1 1.4 copy-start

commit v2 on v1

v2 whole, which is shorter than its diff:
```python
import functools

import jax
import jax.numpy as jnp
from jax import lax
from jax.experimental import pallas as pl
from jax.experimental.pallas import tpu as pltpu
from jax.sharding import PartitionSpec as P

MESH_ID = pl.DeviceIdType.MESH
F32 = jnp.float32
BF16 = jnp.bfloat16

TOK = 96
CAP = 36
D = 2048
BLK = 192
XN = 4
GN = 4
FN = 4
DN = 4
GT = GN * TOK
CHUNK = GN * CAP
ROWS = XN * CHUNK
HALF = 2 * BLK
QUART = BLK // DN
NC = 4
CW = D // NC

NSEM = 192
SPREAD = (2,)


def dot_nt(a, b):
    return lax.dot_general(a, b, (((1,), (1,)), ((), ())), preferred_element_type=F32)


def dot_nn(a, b):
    return lax.dot_general(a, b, (((1,), (0,)), ((), ())), preferred_element_type=F32)


def dot_tn(a, b):
    return lax.dot_general(a, b, (((0,), (0,)), ((), ())), preferred_element_type=F32)


def kernel(
    meta_ref, x_ref, u_ref, wg_ref, wu_ref, wd_ref,
    out_x, out_g, out_u, out_d,
    metas, tok, tab, gsl, snd, rows, wts, gu, dh, dgu, tr, gacc, gsend, grecv,
    red_a, red_b, red_p, red_n, fin, p_own, p_send, p_recv, q, part, core_recv,
    z_send, z_recv, gout, ssem, rsem, lsem,
):
    e = lax.axis_index("expert")
    f = lax.axis_index("fsdp")
    d = lax.axis_index("dp")
    core = lax.rem(e, 2)
    sib_e = e + 1 - 2 * core
    zp_e = e + 2 - 4 * lax.rem(lax.div(e, 2), 2)
    diag_e = zp_e + 1 - 2 * core
    near = f + 1 - 2 * lax.rem(f, 2)
    far = FN - 1 - f
    row_f = near + core * (far - near)
    wgt_f = far + core * (near - far)
    up_d = lax.rem(d + 1, DN)
    dn_d = lax.rem(d + DN - 1, DN)
    op_d = lax.rem(d + 2, DN)

    sib = {"expert": sib_e}
    zp = {"expert": zp_e}
    diag = {"expert": diag_e}
    x_at = [{"expert": lax.rem(e + GN * o, XN * GN)} for o in range(XN)]
    row_y = {"fsdp": row_f}
    wgt_y = {"fsdp": wgt_f}
    d_up = {"dp": up_d}
    d_dn = {"dp": dn_d}

    used = [0]

    def remote(src, dst, dev):
        i = used[0]
        used[0] += 1
        return pltpu.make_async_remote_copy(
            src_ref=src, dst_ref=dst, send_sem=ssem.at[i], recv_sem=rsem.at[i],
            device_id=dev, device_id_type=MESH_ID,
        )

    pending = {}

    def send(src, dst, dev):
        c = remote(src, dst, dev)
        c.start()
        pending[id(c)] = c
        return c

    lused = [0]

    def local_copy(src, dst):
        i = lused[0]
        lused[0] += 1
        c = pltpu.make_async_copy(src, dst, lsem.at[i])
        c.start()
        return c

    toks = (x_ref, u_ref)
    own_tok = [local_copy(toks[a], tok.at[a, pl.ds(0, TOK)]) for a in range(2)]
    weights = (wg_ref, wu_ref, wd_ref)
    own_wts = [local_copy(weights[m], wts.at[pl.ds(m * HALF, BLK)]) for m in range(3)]

    partners = [sib, zp, diag] + x_at[1:] + [row_y, wgt_y, d_up, d_dn]
    barrier = pltpu.get_barrier_semaphore()
    for dev in partners:
        pl.semaphore_signal(barrier, inc=1, device_id=dev, device_id_type=MESH_ID)
    pl.semaphore_wait(barrier, len(partners))

    def quarter(i):
        return pl.ds(pl.multiple_of(i * QUART, QUART), QUART)

    def wts_quarter(m, i):
        return pl.ds(pl.multiple_of(m * HALF + BLK + i * QUART, QUART), QUART)

    meta_c = [send(meta_ref, metas.at[i], dev) for i, dev in enumerate((zp, sib, diag))]
    tok_z = {}
    tok_s = {}

    def send_tokens(a, c):
        cols = pl.ds(c * CW, CW)
        mine = tok.at[a, pl.ds(0, TOK), cols]
        tok_z[a, c] = send(mine, tok.at[a, pl.ds(TOK, TOK), cols], zp)
        tok_s[a, c] = send(mine, tok.at[a, pl.ds(2 * TOK, TOK), cols], sib)

    steps = [(a, c) for a in range(2) for c in range(NC)]
    own_tok[0].wait()
    for step in steps[:2]:
        send_tokens(*step)
    own_tok[1].wait()
    w_y = {}
    for m in range(3):
        own_wts[m].wait()
        if m in SPREAD:
            src = wts.at[pl.ds(pl.multiple_of(m * HALF + d * QUART, QUART), QUART), :]
            w_y[m] = send(src, wts.at[wts_quarter(m, d), :], wgt_y)
        else:
            src = wts.at[pl.ds(m * HALF, BLK)]
            w_y[m] = send(src, wts.at[pl.ds(m * HALF + BLK, BLK)], wgt_y)
    w1 = {}
    w2 = {}
    lo = pl.ds(0, D // 2)
    hi = pl.ds(D // 2, D // 2)

    def weights_first(m):
        w_y[m].wait_recv()
        at = wts_quarter(m, d)
        w1[m] = (
            send(wts.at[at, :], wts.at[at, :], d_up),
            send(wts.at[at, :], wts.at[at, :], d_dn),
        )

    def weights_second(m):
        w1[m][0].wait_recv()
        at = wts_quarter(m, dn_d)
        first_c = send(wts.at[at, lo], wts.at[at, lo], d_up)
        w1[m][1].wait_recv()
        at = wts_quarter(m, up_d)
        w2[m] = (first_c, send(wts.at[at, hi], wts.at[at, hi], d_dn))

    for c in meta_c:
        c.wait_recv()
    lane = lax.broadcasted_iota(jnp.int32, (8, GT), 1)
    meta = meta_ref[...]
    for r in range(1, GN):
        meta = jnp.where(lane >= r * TOK, metas[r - 1], meta)
    source = sum((lane >= r * TOK).astype(F32) for r in range(1, GN))
    relative = lax.broadcasted_iota(jnp.int32, (8, GT), 0)
    expert = lax.rem(e + GN * relative, XN * GN).astype(F32)
    hit0 = meta[0:1] == expert
    hit1 = meta[1:2] == expert
    hit = jnp.logical_or(hit0, hit1)
    t_row = lax.broadcasted_iota(jnp.int32, (GT, GT), 0)
    t_col = lax.broadcasted_iota(jnp.int32, (GT, GT), 1)
    first = sum(jnp.where(t_col >= r * TOK, TOK, 0) for r in range(1, GN))
    before = jnp.logical_and(t_row < t_col, t_row >= first)
    earlier = dot_nn(
        jnp.where(hit, 1.0, 0.0).astype(BF16), jnp.where(before, 1.0, 0.0).astype(BF16)
    )
    target = jnp.where(hit, source * CAP + earlier, -1.0)
    weight = jnp.where(hit0, meta[2:3], jnp.where(hit1, meta[3:4], 0.0))
    slot = lax.broadcasted_iota(jnp.int32, (CHUNK, GT), 0).astype(F32)
    for o in range(XN):
        same = slot == target[o : o + 1]
        at = pl.ds(o * CHUNK, CHUNK)
        tab[at, :] = jnp.where(same, 1.0, 0.0).astype(BF16)
        gates = jnp.sum(jnp.where(same, weight[o : o + 1], 0.0), axis=1, keepdims=True)
        gsl[at, :] = jnp.broadcast_to(gates, (CHUNK, 128))

    x_c = {}
    y_c = {}

    def pick(a, c):
        cols = pl.ds(c * CW, CW)
        picked = dot_nn(tab[...], tok[a, :, cols])
        if a == 1:
            picked = picked * gsl[:, 0:1]
        picked = picked.astype(BF16)
        rows[a, pl.ds(0, CHUNK), cols] = picked[0:CHUNK]
        for o in range(1, XN):
            snd[a, o - 1, :, cols] = picked[o * CHUNK : (o + 1) * CHUNK]

    def send_rows(a, c):
        cols = pl.ds(c * CW, CW)
        for o in (2, 1, 3):
            x_c[a, c, o] = send(
                snd.at[a, o - 1, :, cols],
                rows.at[a, pl.ds((XN - o) * CHUNK, CHUNK), cols],
                x_at[o],
            )

    def pass_on(a, c):
        for o in (1, 3, 2):
            x_c[a, c, o].wait_recv()
        cols = pl.ds(c * CW, CW)
        y_c[a, c] = send(
            rows.at[a, pl.ds(0, ROWS), cols], rows.at[a, pl.ds(ROWS, ROWS), cols], row_y
        )

    def gate_up(s):
        at = pl.ds(s * ROWS, ROWS)

        @pl.loop(0, 3)
        def _(n):
            tile = pl.ds(pl.multiple_of(n * 256, 256), 256)
            gu[at, tile] = dot_nt(rows[0, at, :], wts[tile, :])

    def d_hidden(s):
        if s == 1:
            for c in range(NC):
                need(c)
        at = pl.ds(s * ROWS, ROWS)
        dh[at, :] = dot_nt(rows[1, at, :], wts[pl.ds(2 * HALF, HALF), :])

    def turn(m, at, value):
        turned = value.T
        tr[pl.ds(m * BLK, BLK), at] = turned[BLK:HALF]
        tr[pl.ds((3 + m) * BLK, BLK), at] = turned[0:BLK]

    def make_hidden():
        @pl.loop(0, 2 * ROWS // 128)
        def _(i):
            at = pl.ds(pl.multiple_of(i * 128, 128), 128)
            gate = gu[at, pl.ds(0, HALF)]
            upward = gu[at, pl.ds(HALF, HALF)]
            logistic = jax.nn.sigmoid(gate)
            active = gate * logistic
            slope = logistic * (1.0 + gate * (1.0 - logistic))
            gu[at, pl.ds(0, HALF)] = upward * slope
            gu[at, pl.ds(HALF, HALF)] = active
            turn(2, at, (active * upward).astype(BF16))

    def elementwise(low, high):
        @pl.loop(low, high)
        def _(i):
            at = pl.ds(pl.multiple_of(i * 128, 128), 128)
            dhid = dh[at, :]
            for m in range(2):
                cols = pl.ds(m * HALF, HALF)
                value = (dhid * gu[at, cols]).astype(BF16)
                dgu[at, cols] = value
                turn(m, at, value)

    def wait_weights(m):
        for c in w2[m] if m in SPREAD else (w_y[m],):
            c.wait_recv()

    for k, (a, c) in enumerate(steps):
        if k + 2 < len(steps):
            send_tokens(*steps[k + 2])
        cols = pl.ds(c * CW, CW)
        tok_z[a, c].wait_recv()
        fwd = send(tok.at[a, pl.ds(TOK, TOK), cols], tok.at[a, pl.ds(3 * TOK, TOK), cols], sib)
        tok_s[a, c].wait_recv()
        fwd.wait_recv()
        pick(a, c)
        if k >= 2:
            pass_on(*steps[k - 2])
        send_rows(a, c)
        for m in SPREAD:
            if k == 2 + m:
                weights_first(m)
            if k == 5 + m:
                weights_second(m)
        if k == NC + 2:
            for m in range(2):
                wait_weights(m)
            gate_up(0)
        if k == NC + 3:
            for i in range(NC):
                y_c[0, i].wait_recv()
            gate_up(1)

    parts = [(2, c * CW, CW) for c in range(NC)]
    half_d = D // 2
    parts += [(m, h * half_d, half_d) for h in range(2) for m in range(2)]

    landed = set()

    def need(c):
        if c not in landed:
            y_c[1, c].wait_recv()
            landed.add(c)

    def grads_down(c):
        need(c)
        cols = pl.ds(c * CW, CW)
        gsend[2, :, cols] = dot_nn(tr[pl.ds(2 * BLK, BLK), :], rows[1, :, cols]).astype(BF16)
        send_grads(c)
        gacc[2, :, cols] = dot_nn(tr[pl.ds(5 * BLK, BLK), :], rows[1, :, cols])

    def grads(mine, h):
        @pl.loop(0, half_d // 512)
        def _(n):
            tile = pl.ds(pl.multiple_of(h * half_d + n * 512, 512), 512)
            value = dot_nn(tr[pl.ds(3 * BLK * mine, 2 * BLK), :], rows[0, :, tile])
            for i in range(2):
                one = value[i * BLK : (i + 1) * BLK]
                if mine:
                    gacc[i, :, tile] = one
                else:
                    gsend[i, :, tile] = one.astype(BF16)

    g_c = {}

    def send_grads(j):
        m, low, width = parts[j]
        cols = pl.ds(low, width)
        g_c[j] = send(gsend.at[m, :, cols], grecv.at[m, :, cols], wgt_y)

    p_c = {}

    def partner_rows(c):
        @pl.loop(0, half_d // 512)
        def _(n):
            tile = pl.ds(pl.multiple_of(c * half_d + n * 512, 512), 512)
            p_send[:, tile] = dot_nn(
                dgu[pl.ds(ROWS, ROWS), :], wts[pl.ds(0, 2 * HALF), tile]
            ).astype(BF16)

    def send_partner_rows(c):
        cols = pl.ds(c * half_d, half_d)
        p_c[c] = send(p_send.at[:, cols], p_recv.at[:, cols], row_y)

    r1 = {}
    r2 = {}
    a1 = {}
    a2 = {}

    def split(j):
        m, low, width = parts[j]
        half = width // 2
        return (
            m, pl.ds(low, half), pl.ds(low + half, half), pl.ds(low, width),
            pl.ds(0, half), pl.ds(0, width),
        )

    def reduce_first(j):
        m, low, high, cols, narrow, wide = split(j)
        g_c[j].wait_recv()
        g_c[j].wait_send()
        del pending[id(g_c[j])]

        @pl.loop(0, BLK // 16)
        def _(i):
            at = pl.ds(pl.multiple_of(i * 16, 16), 16)
            gsend[m, at, cols] = (
                gacc[m, at, cols] + grecv[m, at, cols].astype(F32)
            ).astype(BF16)

        r1[j] = (
            send(gsend.at[m, quarter(op_d), low], red_a.at[j, :, narrow], d_up),
            send(gsend.at[m, quarter(op_d), high], red_b.at[j, :, narrow], d_dn),
        )

    def reduce_second(j):
        m, low, high, cols, narrow, wide = split(j)
        r1[j][0].wait_recv()
        at = quarter(up_d)
        gsend[m, at, low] = (gsend[m, at, low].astype(F32) + red_a[j, :, narrow].astype(F32)).astype(BF16)
        first_c = send(gsend.at[m, at, cols], red_p.at[j, :, wide], d_up)
        r1[j][1].wait_recv()
        at = quarter(dn_d)
        gsend[m, at, high] = (gsend[m, at, high].astype(F32) + red_b[j, :, narrow].astype(F32)).astype(BF16)
        r2[j] = (first_c, send(gsend.at[m, at, cols], red_n.at[j, :, wide], d_dn))

    def gather_first(j):
        m, low, high, cols, narrow, wide = split(j)
        r2[j][0].wait_recv()
        r2[j][1].wait_recv()
        at = quarter(d)
        fin[m, at, cols] = (
            gsend[m, at, cols].astype(F32) + red_p[j, :, wide].astype(F32) + red_n[j, :, wide].astype(F32)
        ).astype(BF16)
        a1[j] = (
            send(fin.at[m, at, cols], fin.at[m, at, cols], d_up),
            send(fin.at[m, at, cols], fin.at[m, at, cols], d_dn),
        )

    def gather_second(j):
        m, low, high, cols, narrow, wide = split(j)
        a1[j][0].wait_recv()
        at = quarter(dn_d)
        first_c = send(fin.at[m, at, low], fin.at[m, at, low], d_up)
        a1[j][1].wait_recv()
        at = quarter(up_d)
        a2[j] = (first_c, send(fin.at[m, at, high], fin.at[m, at, high], d_dn))

    outs = (out_g, out_u, out_d)
    done = []

    def finish(j):
        m, low, high, cols, narrow, wide = split(j)
        a2[j][0].wait_recv()
        a2[j][1].wait_recv()
        done.append(local_copy(fin.at[m, :, cols], outs[m].at[:, cols]))

    q_c = {}
    s_c = {}
    z_c = {}

    def own_rows():
        @pl.loop(0, D // 512)
        def _(n):
            tile = pl.ds(pl.multiple_of(n * 512, 512), 512)
            p_own[:, tile] = dot_nn(dgu[pl.ds(0, ROWS), :], wts[pl.ds(0, 2 * HALF), tile])

    def return_rows(c):
        cols = pl.ds(c * half_d, half_d)
        p_c[c].wait_recv()
        p_c[c].wait_send()
        del pending[id(p_c[c])]

        @pl.loop(0, ROWS // 48)
        def _(i):
            at = pl.ds(pl.multiple_of(i * 48, 48), 48)
            p_send[at, cols] = (p_own[at, cols] + p_recv[at, cols].astype(F32)).astype(BF16)

        for k in (2, 1, 3):
            q_c[c, k] = send(
                p_send.at[pl.ds(k * CHUNK, CHUNK), cols],
                q.at[pl.ds((XN - k) * CHUNK, CHUNK), cols],
                x_at[k],
            )
        q[pl.ds(0, CHUNK), cols] = p_send[pl.ds(0, CHUNK), cols]

    def combine(c):
        cols = pl.ds(c * half_d, half_d)
        for k in (1, 3, 2):
            q_c[c, k].wait_recv()

        @pl.loop(0, half_d // 512)
        def _(n):
            tile = pl.ds(pl.multiple_of(c * half_d + n * 512, 512), 512)
            part[:, tile] = dot_tn(tab[...], q[:, tile]).astype(BF16)

        s_c[c] = send(part.at[pl.ds(2 * TOK, 2 * TOK), cols], core_recv.at[:, cols], sib)

    def along_z(c):
        cols = pl.ds(c * half_d, half_d)
        s_c[c].wait_recv()
        z_send[:, cols] = (
            part[pl.ds(TOK, TOK), cols].astype(F32)
            + core_recv[pl.ds(TOK, TOK), cols].astype(F32)
        ).astype(BF16)
        z_c[c] = send(z_send.at[:, cols], z_recv.at[:, cols], zp)

    def tokens_out(c):
        cols = pl.ds(c * half_d, half_d)
        z_c[c].wait_recv()
        gout[:, cols] = (
            part[pl.ds(0, TOK), cols].astype(F32)
            + core_recv[pl.ds(0, TOK), cols].astype(F32)
            + z_recv[:, cols].astype(F32)
        ).astype(BF16)
        done.append(local_copy(gout.at[:, cols], out_x.at[:, cols]))

    wait_weights(2)
    make_hidden()
    grads_down(0)
    pass_on(*steps[-2])
    grads_down(1)
    reduce_first(0)
    reduce_second(0)
    pass_on(*steps[-1])
    d_hidden(0)
    reduce_first(1)
    gather_first(0)
    reduce_second(1)
    gather_second(0)
    grads_down(2)
    elementwise(0, ROWS // 128)
    gather_first(1)
    d_hidden(1)
    reduce_first(2)
    grads_down(3)
    gather_second(1)
    elementwise(ROWS // 128, 2 * ROWS // 128)
    reduce_second(2)
    grads(0, 0)
    send_grads(4)
    reduce_first(3)
    gather_first(2)
    grads(1, 0)
    reduce_second(3)
    send_grads(5)
    partner_rows(1)
    gather_second(2)
    reduce_first(4)
    partner_rows(0)
    gather_first(3)
    send_partner_rows(0)
    reduce_first(5)
    reduce_second(4)
    grads(0, 1)
    reduce_second(5)
    grads(1, 1)
    finish(1)
    gather_first(4)
    gather_second(3)
    send_grads(7)
    own_rows()
    return_rows(0)
    send_grads(6)
    gather_first(5)
    send_partner_rows(1)
    finish(3)
    gather_second(4)
    finish(2)
    finish(0)
    reduce_first(7)
    reduce_first(6)
    reduce_second(7)
    reduce_second(6)
    return_rows(1)
    gather_first(7)
    gather_first(6)
    combine(0)
    along_z(0)
    gather_second(6)
    finish(4)
    gather_second(5)
    gather_second(7)
    combine(1)
    along_z(1)
    tokens_out(0)
    finish(7)
    finish(5)
    finish(6)
    tokens_out(1)
    for c in done:
        c.wait()
    for c in pending.values():
        c.wait_send()


SCRATCH = (
    ((GN - 1, 8, GT), F32),
    ((2, GT, D), BF16),
    ((ROWS, GT), BF16),
    ((ROWS, 128), F32),
    ((2, XN - 1, CHUNK, D), BF16),
    ((2, 2 * ROWS, D), BF16),
    ((3 * HALF, D), BF16),
    ((2 * ROWS, 2 * HALF), F32),
    ((2 * ROWS, HALF), F32),
    ((2 * ROWS, 2 * HALF), BF16),
    ((6 * BLK, 2 * ROWS), BF16),
    ((3, BLK, D), F32),
    ((3, BLK, D), BF16),
    ((3, BLK, D), BF16),
    ((8, QUART, D // 4), BF16),
    ((8, QUART, D // 4), BF16),
    ((8, QUART, D // 2), BF16),
    ((8, QUART, D // 2), BF16),
    ((3, BLK, D), BF16),
    ((ROWS, D), F32),
    ((ROWS, D), BF16),
    ((ROWS, D), BF16),
    ((ROWS, D), BF16),
    ((GT, D), BF16),
    ((2 * TOK, D), BF16),
    ((TOK, D), BF16),
    ((TOK, D), BF16),
    ((TOK, D), BF16),
)


def local(inputs, upstream, gates, routes, w_gate, w_up, w_down):
    meta = jnp.concatenate(
        [routes.T.astype(F32), gates.T, jnp.zeros((4, TOK), F32)], axis=0
    )
    meta = jnp.tile(meta, (1, GN))
    anywhere = pl.BlockSpec(memory_space=pl.ANY)
    outs = pl.pallas_call(
        kernel,
        out_shape=(
            jax.ShapeDtypeStruct((TOK, D), BF16),
            jax.ShapeDtypeStruct((BLK, D), BF16),
            jax.ShapeDtypeStruct((BLK, D), BF16),
            jax.ShapeDtypeStruct((BLK, D), BF16),
        ),
        in_specs=[pl.BlockSpec(memory_space=pltpu.VMEM)] + [anywhere] * 5,
        out_specs=[anywhere] * 4,
        scratch_shapes=[pltpu.VMEM(shape, dtype) for shape, dtype in SCRATCH]
        + [
            pltpu.SemaphoreType.DMA((NSEM,)),
            pltpu.SemaphoreType.DMA((NSEM,)),
            pltpu.SemaphoreType.DMA((16,)),
        ],
        compiler_params=pltpu.CompilerParams(
            collective_id=0, has_side_effects=True, vmem_limit_bytes=62 * 2**20
        ),
        name="expert_backward",
    )(meta, inputs, upstream, w_gate[0], w_up[0], w_down[0])
    return outs[0], outs[1][None], outs[2][None], outs[3][None]


def solution(mesh):
    tokens = P(("expert", "fsdp", "dp"), None)
    hidden = P("expert", "fsdp", None)
    return jax.shard_map(
        local,
        mesh=mesh,
        in_specs=(tokens, tokens, tokens, tokens, hidden, hidden, hidden),
        out_specs=(tokens, hidden, hidden, hidden),
        check_vma=False,
    )
```

time: 226 us -> 190 us (0.84)
  Pallas kernels: 217 us -> 181 us
    pallas_call x1, Pallas kernels: 217 us -> 181 us  [local(): pl.pallas_call(kernel, out_shape=(jax.ShapeDtypeStruct((TOK, D), BF16), j...]
where the time goes in v2:
time: 190 us; the launch traced here: 189 us
  Pallas kernels  181 us (95%)
  local copies, waits for them, and re-layouts  7.6 us (4%)
    pallas_call x1, Pallas kernels, local(): pl.pallas_call(kernel, out_shape=(jax.ShapeDtypeStruct((TOK, D), BF16), j...  181 us
    unnamed x14, local copies, waits for them, and re-layouts  6.83 us

profile of v2, /device:TPU:1, one launch (start us, length us, event | category | flops | bytes accessed | tf_op | source)
XLA Modules:
  0.0 189.4 jit_solution(16544753725735533797)
XLA Ops:
  0.6 0.0 copy-start.3
  0.7 0.1 pad.2.clone
  0.7 0.6 copy-done.3
  1.3 0.0 copy-start.4
  1.3 0.7 copy-done.4
  2.0 0.1 maximum_maximum_fusion
  2.1 0.7 tile.10.meta_ref
  2.8 181.1 %expert_backward.1 = (bf16[96,2048]{1,0:T(8,128)(2,1)}, bf16[192,2048]{1,0:T(8,128)(2,1)}, bf16[192,2048]{1,0:T(8,128)(2,1)}, bf16[192,2048]{1,0:T(8,128)(2,1)}) custom-call(f32[8,384]{1,0:T(8,128)} %tile.10.meta_ref, bf16[96,2048]{1,0:T(8,128)(2,1)} %x_ref.1, bf16[96,2048]{1,0:T(8,128)(2,1)} %u_ref.1, bf16[192,2048]{1,0:T(8,128)(2,1)} %bitcast.12, ...), custom_call_target="tpu_custom_call" | custom-call | tf_op jit(solution)/shard_map/expert_backward/pallas_call | solution.py:600
  183.9 0.0 copy-start.2
  183.9 1.8 copy.15
  185.7 0.0 copy-done.2
  185.7 0.0 copy-start.1
  185.7 0.9 copy.16
  186.6 0.5 copy-done.1
  187.1 0.0 copy-start
  187.1 0.9 copy.17
  188.0 0.5 copy-done
  188.5 0.9 copy.18
  (3 shorter events, 0.0 us)
Async XLA Ops:
  0.6 0.7 copy-start.3
  1.3 0.7 copy-start.4
  183.9 1.9 copy-start.2
  185.7 1.4 copy-start.1
  187.1 1.4 copy-start

commit v3 on v2

--- a/solution.py
+++ b/solution.py
@@ -25,10 +25,14 @@
 HALF = 2 * BLK
 QUART = BLK // DN
 NC = 4
-CW = D // NC
+CUTS = ((0, 256, 768, 1280, 2048), (0, 768, 1280, 1792, 2048))
 
 NSEM = 192
 SPREAD = (2,)
+
+
+def chunk(a, c):
+    return pl.ds(CUTS[a][c], CUTS[a][c + 1] - CUTS[a][c])
 
 
 def dot_nt(a, b):
@@ -123,7 +127,7 @@
     tok_s = {}
 
     def send_tokens(a, c):
-        cols = pl.ds(c * CW, CW)
+        cols = chunk(a, c)
         mine = tok.at[a, pl.ds(0, TOK), cols]
         tok_z[a, c] = send(mine, tok.at[a, pl.ds(TOK, TOK), cols], zp)
         tok_s[a, c] = send(mine, tok.at[a, pl.ds(2 * TOK, TOK), cols], sib)
@@ -196,7 +200,7 @@
     y_c = {}
 
     def pick(a, c):
-        cols = pl.ds(c * CW, CW)
+        cols = chunk(a, c)
         picked = dot_nn(tab[...], tok[a, :, cols])
         if a == 1:
             picked = picked * gsl[:, 0:1]
@@ -206,7 +210,7 @@
             snd[a, o - 1, :, cols] = picked[o * CHUNK : (o + 1) * CHUNK]
 
     def send_rows(a, c):
-        cols = pl.ds(c * CW, CW)
+        cols = chunk(a, c)
         for o in (2, 1, 3):
             x_c[a, c, o] = send(
                 snd.at[a, o - 1, :, cols],
@@ -217,7 +221,7 @@
     def pass_on(a, c):
         for o in (1, 3, 2):
             x_c[a, c, o].wait_recv()
-        cols = pl.ds(c * CW, CW)
+        cols = chunk(a, c)
         y_c[a, c] = send(
             rows.at[a, pl.ds(0, ROWS), cols], rows.at[a, pl.ds(ROWS, ROWS), cols], row_y
         )
@@ -273,15 +277,15 @@
     for k, (a, c) in enumerate(steps):
         if k + 2 < len(steps):
             send_tokens(*steps[k + 2])
-        cols = pl.ds(c * CW, CW)
+        cols = chunk(a, c)
         tok_z[a, c].wait_recv()
         fwd = send(tok.at[a, pl.ds(TOK, TOK), cols], tok.at[a, pl.ds(3 * TOK, TOK), cols], sib)
         tok_s[a, c].wait_recv()
         fwd.wait_recv()
         pick(a, c)
+        send_rows(a, c)
         if k >= 2:
             pass_on(*steps[k - 2])
-        send_rows(a, c)
         for m in SPREAD:
             if k == 2 + m:
                 weights_first(m)
@@ -296,7 +300,7 @@
                 y_c[0, i].wait_recv()
             gate_up(1)
 
-    parts = [(2, c * CW, CW) for c in range(NC)]
+    parts = [(2, CUTS[1][c], CUTS[1][c + 1] - CUTS[1][c]) for c in range(NC)]
     half_d = D // 2
     parts += [(m, h * half_d, half_d) for h in range(2) for m in range(2)]
 
@@ -309,7 +313,7 @@
 
     def grads_down(c):
         need(c)
-        cols = pl.ds(c * CW, CW)
+        cols = chunk(1, c)
         gsend[2, :, cols] = dot_nn(tr[pl.ds(2 * BLK, BLK), :], rows[1, :, cols]).astype(BF16)
         send_grads(c)
         gacc[2, :, cols] = dot_nn(tr[pl.ds(5 * BLK, BLK), :], rows[1, :, cols])
@@ -483,76 +487,76 @@
     wait_weights(2)
     make_hidden()
     grads_down(0)
+    grads_down(1)
     pass_on(*steps[-2])
-    grads_down(1)
     reduce_first(0)
+    reduce_first(1)
     reduce_second(0)
     pass_on(*steps[-1])
     d_hidden(0)
-    reduce_first(1)
+    elementwise(0, ROWS // 128)
+    reduce_second(1)
+    grads_down(2)
     gather_first(0)
-    reduce_second(1)
-    gather_second(0)
-    grads_down(2)
-    elementwise(0, ROWS // 128)
+    d_hidden(1)
+    elementwise(ROWS // 128, 2 * ROWS // 128)
     gather_first(1)
-    d_hidden(1)
-    reduce_first(2)
     grads_down(3)
-    gather_second(1)
-    elementwise(ROWS // 128, 2 * ROWS // 128)
-    reduce_second(2)
     grads(0, 0)
     send_grads(4)
+    reduce_first(2)
+    partner_rows(1)
+    gather_second(0)
     reduce_first(3)
-    gather_first(2)
     grads(1, 0)
+    send_grads(5)
+    reduce_second(2)
+    grads(0, 1)
     reduce_second(3)
-    send_grads(5)
-    partner_rows(1)
-    gather_second(2)
+    grads(1, 1)
     reduce_first(4)
     partner_rows(0)
+    send_grads(7)
+    gather_second(1)
+    reduce_first(5)
+    send_grads(6)
+    reduce_second(4)
     gather_first(3)
+    reduce_first(7)
     send_partner_rows(0)
-    reduce_first(5)
-    reduce_second(4)
-    grads(0, 1)
+    gather_first(2)
     reduce_second(5)
-    grads(1, 1)
+    own_rows()
+    gather_first(4)
+    reduce_second(7)
     finish(1)
-    gather_first(4)
+    reduce_first(6)
+    send_partner_rows(1)
+    gather_first(5)
+    return_rows(0)
+    gather_second(2)
     gather_second(3)
-    send_grads(7)
-    own_rows()
-    return_rows(0)
-    send_grads(6)
-    gather_first(5)
-    send_partner_rows(1)
-    finish(3)
+    return_rows(1)
+    reduce_second(6)
+    gather_first(7)
+    gather_second(5)
     gather_second(4)
-    finish(2)
-    finish(0)
-    reduce_first(7)
-    reduce_first(6)
-    reduce_second(7)
-    reduce_second(6)
-    return_rows(1)
-    gather_first(7)
-    gather_first(6)
     combine(0)
     along_z(0)
-    gather_second(6)
+    gather_first(6)
+    finish(2)
+    finish(5)
     finish(4)
-    gather_second(5)
+    combine(1)
     gather_second(7)
-    combine(1)
     along_z(1)
     tokens_out(0)
+    finish(3)
     finish(7)
-    finish(5)
+    finish(0)
+    gather_second(6)
+    tokens_out(1)
     finish(6)
-    tokens_out(1)
     for c in done:
         c.wait()
     for c in pending.values():

time: 190 us -> 185 us (0.974)
  Pallas kernels: 181 us -> 176 us
    pallas_call x1, Pallas kernels: 181 us -> 176 us  [local(): pl.pallas_call(kernel, out_shape=(jax.ShapeDtypeStruct((TOK, D), BF16), j...]
where the time goes in v3:
time: 185 us; the launch traced here: 184 us
  Pallas kernels  176 us (95%)
  local copies, waits for them, and re-layouts  7.6 us (4%)
    pallas_call x1, Pallas kernels, local(): pl.pallas_call(kernel, out_shape=(jax.ShapeDtypeStruct((TOK, D), BF16), j...  176 us
    unnamed x14, local copies, waits for them, and re-layouts  6.83 us

profile of v3, /device:TPU:1, one launch (start us, length us, event | category | flops | bytes accessed | tf_op | source)
XLA Modules:
  0.0 184.4 jit_solution(15789903456934662464)
XLA Ops:
  0.6 0.0 copy-start.3
  0.7 0.1 pad.2.clone
  0.7 0.6 copy-done.3
  1.3 0.0 copy-start.4
  1.3 0.7 copy-done.4
  2.0 0.1 maximum_maximum_fusion
  2.1 0.7 tile.10.meta_ref
  2.8 176.0 %expert_backward.1 = (bf16[96,2048]{1,0:T(8,128)(2,1)}, bf16[192,2048]{1,0:T(8,128)(2,1)}, bf16[192,2048]{1,0:T(8,128)(2,1)}, bf16[192,2048]{1,0:T(8,128)(2,1)}) custom-call(f32[8,384]{1,0:T(8,128)} %tile.10.meta_ref, bf16[96,2048]{1,0:T(8,128)(2,1)} %x_ref.1, bf16[96,2048]{1,0:T(8,128)(2,1)} %u_ref.1, bf16[192,2048]{1,0:T(8,128)(2,1)} %bitcast.12, ...), custom_call_target="tpu_custom_call" | custom-call | tf_op jit(solution)/shard_map/expert_backward/pallas_call | solution.py:604
  178.8 0.0 copy-start.2
  178.8 1.8 copy.15
  180.6 0.0 copy-done.2
  180.6 0.0 copy-start.1
  180.6 0.9 copy.16
  181.5 0.5 copy-done.1
  182.1 0.0 copy-start
  182.1 0.9 copy.17
  182.9 0.5 copy-done
  183.5 0.9 copy.18
  (3 shorter events, 0.0 us)
Async XLA Ops:
  0.6 0.7 copy-start.3
  1.3 0.7 copy-start.4
  178.8 1.9 %copy-start.2 = (bf16[192,2048]{1,0:T(8,128)(2,1)S(1)}, bf16[192,2048]{1,0:T(8,128)(2,1)}, u32[]{:S(2)}) copy-start(bf16[192,2048]{1,0:T(8,128)(2,1)} %get-tuple-element.9) | copy-start | bytes 2359300
  180.6 1.4 copy-start.1
  182.1 1.4 copy-start

commit v4 on v3

--- a/solution.py
+++ b/solution.py
@@ -27,7 +27,7 @@
 NC = 4
 CUTS = ((0, 256, 768, 1280, 2048), (0, 768, 1280, 1792, 2048))
 
-NSEM = 192
+NSEM = 224
 SPREAD = (2,)
 
 
@@ -228,6 +228,12 @@
 
     def gate_up(s):
         at = pl.ds(s * ROWS, ROWS)
+        if s == 0:
+            wait_weights(0)
+            wait_weights(1)
+        else:
+            for c in range(NC):
+                y_c[0, c].wait_recv()
 
         @pl.loop(0, 3)
         def _(n):
@@ -235,7 +241,9 @@
             gu[at, tile] = dot_nt(rows[0, at, :], wts[tile, :])
 
     def d_hidden(s):
-        if s == 1:
+        if s == 0:
+            wait_weights(2)
+        else:
             for c in range(NC):
                 need(c)
         at = pl.ds(s * ROWS, ROWS)
@@ -274,31 +282,23 @@
         for c in w2[m] if m in SPREAD else (w_y[m],):
             c.wait_recv()
 
-    for k, (a, c) in enumerate(steps):
-        if k + 2 < len(steps):
-            send_tokens(*steps[k + 2])
+    fwd = {}
+
+    def forward(k):
+        a, c = steps[k]
         cols = chunk(a, c)
         tok_z[a, c].wait_recv()
-        fwd = send(tok.at[a, pl.ds(TOK, TOK), cols], tok.at[a, pl.ds(3 * TOK, TOK), cols], sib)
+        fwd[k] = send(
+            tok.at[a, pl.ds(TOK, TOK), cols], tok.at[a, pl.ds(3 * TOK, TOK), cols], sib
+        )
+
+    def front(k):
+        a, c = steps[k]
         tok_s[a, c].wait_recv()
-        fwd.wait_recv()
+        fwd[k].wait_recv()
         pick(a, c)
         send_rows(a, c)
-        if k >= 2:
-            pass_on(*steps[k - 2])
-        for m in SPREAD:
-            if k == 2 + m:
-                weights_first(m)
-            if k == 5 + m:
-                weights_second(m)
-        if k == NC + 2:
-            for m in range(2):
-                wait_weights(m)
-            gate_up(0)
-        if k == NC + 3:
-            for i in range(NC):
-                y_c[0, i].wait_recv()
-            gate_up(1)
+
 
     parts = [(2, CUTS[1][c], CUTS[1][c + 1] - CUTS[1][c]) for c in range(NC)]
     half_d = D // 2
@@ -484,77 +484,108 @@
         ).astype(BF16)
         done.append(local_copy(gout.at[:, cols], out_x.at[:, cols]))
 
-    wait_weights(2)
+    forward(0)
+    send_tokens(*steps[2])
+    send_tokens(*steps[3])
+    forward(1)
+    front(0)
+    front(1)
+    send_tokens(*steps[4])
+    forward(2)
+    send_tokens(*steps[5])
+    front(2)
+    pass_on(*steps[0])
+    send_tokens(*steps[6])
+    forward(3)
+    front(3)
+    pass_on(*steps[1])
+    forward(4)
+    pass_on(*steps[2])
+    send_tokens(*steps[7])
+    weights_first(2)
+    forward(5)
+    front(4)
+    pass_on(*steps[3])
+    weights_second(2)
+    front(5)
+    gate_up(0)
+    forward(7)
+    pass_on(*steps[4])
+    pass_on(*steps[5])
+    gate_up(1)
+    forward(6)
     make_hidden()
+    front(6)
     grads_down(0)
     grads_down(1)
-    pass_on(*steps[-2])
+    pass_on(*steps[6])
+    front(7)
     reduce_first(0)
     reduce_first(1)
     reduce_second(0)
-    pass_on(*steps[-1])
+    pass_on(*steps[7])
     d_hidden(0)
     elementwise(0, ROWS // 128)
     reduce_second(1)
     grads_down(2)
     gather_first(0)
+    grads_down(3)
     d_hidden(1)
+    gather_first(1)
     elementwise(ROWS // 128, 2 * ROWS // 128)
-    gather_first(1)
-    grads_down(3)
     grads(0, 0)
+    reduce_first(3)
     send_grads(4)
     reduce_first(2)
+    grads(1, 0)
+    gather_second(0)
+    grads(0, 1)
+    send_grads(5)
+    reduce_second(3)
+    gather_second(1)
     partner_rows(1)
-    gather_second(0)
-    reduce_first(3)
-    grads(1, 0)
-    send_grads(5)
     reduce_second(2)
-    grads(0, 1)
-    reduce_second(3)
-    grads(1, 1)
     reduce_first(4)
     partner_rows(0)
     send_grads(7)
-    gather_second(1)
+    gather_first(3)
+    gather_first(2)
+    send_grads(6)
+    grads(1, 1)
+    finish(0)
     reduce_first(5)
-    send_grads(6)
     reduce_second(4)
-    gather_first(3)
+    reduce_first(6)
+    send_partner_rows(0)
     reduce_first(7)
-    send_partner_rows(0)
-    gather_first(2)
+    own_rows()
+    gather_second(2)
     reduce_second(5)
-    own_rows()
+    reduce_second(7)
     gather_first(4)
-    reduce_second(7)
+    return_rows(0)
+    gather_second(3)
+    send_partner_rows(1)
     finish(1)
-    reduce_first(6)
-    send_partner_rows(1)
+    reduce_second(6)
     gather_first(5)
-    return_rows(0)
-    gather_second(2)
-    gather_second(3)
+    gather_first(7)
     return_rows(1)
-    reduce_second(6)
-    gather_first(7)
+    combine(0)
+    gather_first(6)
+    along_z(0)
+    gather_second(4)
     gather_second(5)
-    gather_second(4)
-    combine(0)
-    along_z(0)
-    gather_first(6)
-    finish(2)
-    finish(5)
-    finish(4)
     combine(1)
     gather_second(7)
+    finish(2)
     along_z(1)
+    finish(5)
+    finish(7)
+    finish(4)
+    finish(3)
+    gather_second(6)
     tokens_out(0)
-    finish(3)
-    finish(7)
-    finish(0)
-    gather_second(6)
     tokens_out(1)
     finish(6)
     for c in done:

time: 185 us -> 186 us (level)
  no operation moved by 1% of the time
where the time goes in v4:
time: 186 us; the launch traced here: 185 us
  Pallas kernels  177 us (95%)
  local copies, waits for them, and re-layouts  7.6 us (4%)
    pallas_call x1, Pallas kernels, local(): pl.pallas_call(kernel, out_shape=(jax.ShapeDtypeStruct((TOK, D), BF16), j...  177 us
    unnamed x14, local copies, waits for them, and re-layouts  6.83 us

profile of v4, /device:TPU:1, one launch (start us, length us, event | category | flops | bytes accessed | tf_op | source)
XLA Modules:
  0.0 185.5 jit_solution(6843990052178128653)
XLA Ops:
  0.6 0.0 copy-start.3
  0.7 0.1 pad.2.clone
  0.7 0.6 copy-done.3
  1.3 0.0 copy-start.4
  1.3 0.7 copy-done.4
  2.0 0.1 maximum_maximum_fusion
  2.1 0.7 tile.10.meta_ref
  2.8 177.1 %expert_backward.1 = (bf16[96,2048]{1,0:T(8,128)(2,1)}, bf16[192,2048]{1,0:T(8,128)(2,1)}, bf16[192,2048]{1,0:T(8,128)(2,1)}, bf16[192,2048]{1,0:T(8,128)(2,1)}) custom-call(f32[8,384]{1,0:T(8,128)} %tile.10.meta_ref, bf16[96,2048]{1,0:T(8,128)(2,1)} %x_ref.1, bf16[96,2048]{1,0:T(8,128)(2,1)} %u_ref.1, bf16[192,2048]{1,0:T(8,128)(2,1)} %bitcast.12, ...), custom_call_target="tpu_custom_call" | custom-call | tf_op jit(solution)/shard_map/expert_backward/pallas_call | solution.py:635
  179.9 0.0 copy-start.2
  179.9 1.8 copy.15
  181.8 0.0 copy-done.2
  181.8 0.0 copy-start.1
  181.8 0.9 copy.16
  182.6 0.5 copy-done.1
  183.2 0.0 copy-start
  183.2 0.9 copy.17
  184.1 0.5 copy-done
  184.6 0.9 copy.18
  (3 shorter events, 0.0 us)
Async XLA Ops:
  0.6 0.7 copy-start.3
  1.3 0.7 copy-start.4
  179.9 1.9 copy-start.2
  181.8 1.4 copy-start.1
  183.2 1.4 copy-start
